TPU v7x, 256 devices: a whole 4x4x8 slice. The times are simulated.
256 devices in a mesh: orient: 64 (over x, y_hi, z), dom: 4 (over y_lo, core).
Axes of the slice: x: 4, y: 4 (y_hi: 2, y_lo: 2; y = y_hi * 2 + y_lo), z: 8, core: 2. Of those that a mesh axis runs over, the one named last changes fastest.
Arguments:
- images: bfloat16 [256, 2, 4096], P(('orient', 'dom')), may hold values from -6 to 6
- offsets: int32 [256, 9, 2], P(('orient', 'dom')), may hold values from -5 to 5, as said below
- groups: int32 [256], P(('orient', 'dom')), may hold values from 0 to 7
- defocus: int32 [256], P(('orient', 'dom')), may hold values from 0 to 63
- refs: bfloat16 [8192, 2, 4096], P('orient'), may hold values from -2 to 2
- log_prior: float32 [8192], P('orient'), may hold values from -4 to 4
- noise_inv: float32 [8, 4096], replicated, may hold values from 0.030029297 to 0.12011719
- ctf_table: float32 [64, 4096], replicated, may hold values from 0.05 to 1
Outputs:
- data_sum: float32 [8192, 2, 4096], P('orient', None, 'dom')
- weight_sum: float32 [8192, 4096], P('orient', 'dom')
- evidence: float32 [256], P(('orient', 'dom'))
Inputs may be any that keep to these rules, and one draw needn't show every extreme that they name: offsets[i, t] = centre[i] + (2 (t mod 3) - 2, 2 (t // 3) - 2) for one centre of each particle.
All inputs are finite; a program needn't handle non-finite values.
Results may differ from a plain program's by a relative error of at most 0.025.
Values may be sent and summed in bfloat16 or wider, within the bound.
No kernel may reach another device: no remote copies, remote signals or barrier semaphores. Data moves between devices by JAX's collectives and lax.ppermute only.
A program may use at most 64 MiB of HBM per device.

v0:
```python
import math
import jax
import jax.numpy as jnp
from jax import lax
from jax.sharding import PartitionSpec as P

SIDE = 64
TWO_PI = 2.0 * math.pi
TRANS_VAR = 8.0
CONTRACT_ROWS = (((0,), (0,)), ((), ()))
CONTRACT_LAST = (((1,), (1,)), ((), ()))


def frequencies(count):
    pixel = jnp.arange(count, dtype=jnp.int32)
    half = SIDE // 2
    return ((pixel % SIDE + half) % SIDE - half, (pixel // SIDE + half) % SIDE - half)


def shifted(weighted, shift_x, shift_y, freq_x, freq_y):
    turns = (shift_x[:, None] * freq_x[None, :] + shift_y[:, None] * freq_y[None, :]) % SIDE
    angle = turns.astype(jnp.float32) * (TWO_PI / SIDE)
    cosine = jnp.cos(angle)
    sine = jnp.sin(angle)
    real_part = weighted[:, 0].astype(jnp.float32)
    imag_part = weighted[:, 1].astype(jnp.float32)
    new_real = real_part * cosine + imag_part * sine
    new_imag = imag_part * cosine - real_part * sine
    return jnp.concatenate([new_real, new_imag], axis=1).astype(jnp.bfloat16)


def lookup(index, table):
    picks = (index[:, None] == jnp.arange(table.shape[0], dtype=jnp.int32)[None, :]).astype(
        jnp.float32
    )
    return jnp.dot(picks, table, precision=lax.Precision.HIGHEST)


def on_device(images, offsets, groups, defocus, refs, log_prior, noise_inv, ctf_table):
    own = images.shape[0]
    pixels = images.shape[2]
    count_refs = refs.shape[0]
    trans = offsets.shape[1]
    scale = (
        25.0
        * (count_refs * lax.axis_size("orient"))
        / (own * lax.axis_size("orient") * lax.axis_size("dom"))
    )
    meta = jnp.concatenate(
        [offsets.reshape(own, 2 * trans), groups[:, None], defocus[:, None]], axis=1
    ).astype(jnp.bfloat16)
    gathered, meta_all = (
        lax.all_gather(images, "orient", axis=0, tiled=True),
        lax.all_gather(meta, "orient", axis=0, tiled=True),
    )
    codes = meta_all.astype(jnp.int32)
    shift_x = codes[:, 0 : 2 * trans : 2]
    shift_y = codes[:, 1 : 2 * trans : 2]
    noise_row = lookup(codes[:, 2 * trans], noise_inv)
    ctf_row = lookup(codes[:, 2 * trans + 1], ctf_table)
    product = noise_row * ctf_row
    weighted = (gathered.astype(jnp.float32) * product[:, None, :]).astype(jnp.bfloat16)
    ctf_power = (product * ctf_row).astype(jnp.bfloat16)
    ref_flat = refs.reshape(count_refs, 2 * pixels)
    real_ref = refs[:, 0].astype(jnp.float32)
    imag_ref = refs[:, 1].astype(jnp.float32)
    power = (real_ref * real_ref + imag_ref * imag_ref).astype(jnp.bfloat16)
    self_term = lax.dot_general(ctf_power, power, CONTRACT_LAST, preferred_element_type=jnp.float32)
    freq_x, freq_y = frequencies(pixels)
    crosses = []
    moved_list = []
    for step in range(trans):
        moved = shifted(weighted, shift_x[:, step], shift_y[:, step], freq_x, freq_y)
        moved_list.append(moved)
        crosses.append(
            lax.dot_general(moved, ref_flat, CONTRACT_LAST, preferred_element_type=jnp.float32)
        )
    cross = jnp.stack(crosses)
    prior = -((shift_x * shift_x + shift_y * shift_y).astype(jnp.float32) / (2.0 * TRANS_VAR))
    score = cross - 0.5 * self_term[None, :, :] + prior.T[:, :, None] + log_prior[None, None, :]
    local_top = jnp.max(score, axis=(0, 2))
    top = lax.pmax(local_top, "orient")
    mass = lax.psum(jnp.sum(jnp.exp(score - top[None, :, None]), axis=(0, 2)), "orient")
    evidence = top + jnp.log(mass)
    post = jnp.exp(score - evidence[None, :, None]).astype(jnp.bfloat16)
    post_sum = jnp.sum(post.astype(jnp.float32), axis=0).astype(jnp.bfloat16)
    data_acc = jnp.zeros((count_refs, 2 * pixels), jnp.float32)
    for step in range(trans):
        data_acc = data_acc + lax.dot_general(
            post[step], moved_list[step], CONTRACT_ROWS, preferred_element_type=jnp.float32
        )
    weight_acc = lax.dot_general(
        post_sum, ctf_power, CONTRACT_ROWS, preferred_element_type=jnp.float32
    )
    stacked = (
        jnp.concatenate([data_acc.reshape(count_refs, 2, pixels), weight_acc[:, None, :]], axis=1)
        * scale
    )
    shares = lax.psum_scatter(
        stacked.astype(jnp.bfloat16), "dom", scatter_dimension=2, tiled=True
    ).astype(jnp.float32)
    data_sum = shares[:, 0:2]
    weight_sum = shares[:, 2]
    own_evidence = lax.dynamic_slice_in_dim(evidence, lax.axis_index("orient") * own, own, 0)
    return (data_sum, weight_sum, own_evidence)


def solution(mesh):
    placed = (
        P(("orient", "dom"), None, None),
        P(("orient", "dom"), None, None),
        P(("orient", "dom")),
        P(("orient", "dom")),
        P("orient", None, None),
        P("orient"),
        P(),
        P(),
    )
    return jax.shard_map(
        on_device,
        mesh=mesh,
        in_specs=placed,
        out_specs=(P("orient", None, "dom"), P("orient", "dom"), P(("orient", "dom"))),
        check_vma=False,
    )
```

profile of v0, /device:TPU:1, one launch (start us, length us, event | category | flops | bytes accessed | tf_op | source)
XLA Modules:
  0.0 670.9 jit_solution(16551002698185999900)
XLA Ops:
  7.2 0.7 all-gather.3.cloned.1.call-update
  8.0 0.7 convert.69
  10.2 156.5 %all-gather = bf16[64,1,20]{2,1,0:T(2,128)(2,1)S(1)} all-gather(bf16[1,1,20]{2,1,0:T(2,128)(2,1)S(1)} %maximum_bitcast_fusion), channel_id=1, replica_groups=mesh['orient'=64,'dom'=4] {'orient'}, dimensions={0}, use_global_device_ids=true | all-gather | bytes 2600 | tf_op jit(solution)/shard_map/all_gather | solution.py:54
  166.9 4.3 copy.40
  171.2 0.6 fusion.97
  172.1 0.6 multiply_convert_fusion.1
  172.9 5.1 fusion.130
  178.0 2.4 convolution_multiply_fusion.1
  180.4 2.0 multiply_convert_fusion
  182.4 4.7 fusion.40
  187.1 0.9 fusion.9
  188.0 9.0 %fusion.72 = (bf16[64,4096]{1,0:T(8,128)(2,1)S(1)}, bf16[64,4096]{1,0:T(8,128)(2,1)S(1)}, bf16[64,4096]{1,0:T(8,128)(2,1)S(1)}, bf16[64,4096]{1,0:T(8,128)(2,1)S(1)}) fusion(s32[4096]{0:T(1024)S(1)} %get-tuple-element.68, s32[64]{0:T(128)S(1)} %get-tuple-element.56, s32[4096]{0:T(1024)S(1)} %get-tuple-element.67, s32[64]{0:T(128)S(1)} %get-tuple-element.77, ...), kind=kLoop, calls=%fused_computation.158 | loop fusion | flops 13107200 | bytes 3179520 | tf_op jit(solution)/shard_map/convert.3
  197.1 0.8 fusion.8
  197.9 9.6 %fusion.68 = (bf16[64,4096]{1,0:T(8,128)(2,1)S(1)}, bf16[64,4096]{1,0:T(8,128)(2,1)S(1)}, bf16[64,4096]{1,0:T(8,128)(2,1)S(1)}, bf16[64,4096]{1,0:T(8,128)(2,1)S(1)}) fusion(s32[4096]{0:T(1024)S(1)} %get-tuple-element.68, s32[64]{0:T(128)S(1)} %get-tuple-element.57, s32[4096]{0:T(1024)S(1)} %get-tuple-element.67, s32[64]{0:T(128)S(1)} %get-tuple-element.76, ...), kind=kLoop, calls=%fused_computation.154 | loop fusion | flops 13107200 | bytes 3179520 | tf_op jit(solution)/shard_map/convert.5
  207.6 0.8 fusion.7
  208.4 9.0 %fusion.64 = (bf16[64,4096]{1,0:T(8,128)(2,1)S(1)}, bf16[64,4096]{1,0:T(8,128)(2,1)S(1)}, bf16[64,4096]{1,0:T(8,128)(2,1)S(1)}, bf16[64,4096]{1,0:T(8,128)(2,1)S(1)}) fusion(s32[4096]{0:T(1024)S(1)} %get-tuple-element.68, s32[64]{0:T(128)S(1)} %get-tuple-element.58, s32[4096]{0:T(1024)S(1)} %get-tuple-element.67, s32[64]{0:T(128)S(1)} %get-tuple-element.75, ...), kind=kLoop, calls=%fused_computation.150 | loop fusion | flops 13107200 | bytes 3179520 | tf_op jit(solution)/shard_map/convert.7
  217.5 0.8 fusion.6
  218.4 9.2 %fusion.60 = (bf16[64,4096]{1,0:T(8,128)(2,1)S(1)}, bf16[64,4096]{1,0:T(8,128)(2,1)S(1)}, bf16[64,4096]{1,0:T(8,128)(2,1)S(1)}, bf16[64,4096]{1,0:T(8,128)(2,1)S(1)}) fusion(s32[4096]{0:T(1024)S(1)} %get-tuple-element.68, s32[64]{0:T(128)S(1)} %get-tuple-element.59, s32[4096]{0:T(1024)S(1)} %get-tuple-element.67, s32[64]{0:T(128)S(1)} %get-tuple-element.74, ...), kind=kLoop, calls=%fused_computation.146 | loop fusion | flops 13107200 | bytes 3179520 | tf_op jit(solution)/shard_map/convert.9
  227.6 0.8 fusion.5
  228.5 0.8 fusion.4
  229.4 0.8 fusion.3
  230.3 0.8 fusion.2
  231.2 0.9 fusion.1
  232.3 148.6 %pmax.7 = f32[64]{0:T(128)S(1)} all-reduce(f32[64]{0:T(128)S(1)} %fusion.96), channel_id=1, replica_groups=mesh['orient'=64,'dom'=4] {'orient'}, use_global_device_ids=true, to_apply=%region_1.2 | all-reduce | flops 64 | bytes 512 | tf_op jit(solution)/shard_map/pmax | solution.py:82
  381.2 150.6 %psum.7 = f32[64]{0:T(128)S(1)} all-reduce(f32[64]{0:T(128)S(1)} %exponential_reduce_fusion), channel_id=1, replica_groups=mesh['orient'=64,'dom'=4] {'orient'}, use_global_device_ids=true, to_apply=%region_3.4 | all-reduce | flops 64 | bytes 512 | tf_op jit(solution)/shard_map/psum | solution.py:83
  532.0 0.7 fusion.77
  532.7 0.3 copy-done.14
  533.2 0.7 convolution_add_fusion.7
  533.9 0.3 copy-done.22
  534.4 0.7 convolution_add_fusion.6
  535.1 0.3 copy-done.26
  535.6 0.7 convolution_add_fusion.5
  536.3 0.3 copy-done.34
  536.8 0.7 convolution_add_fusion.4
  537.5 0.3 copy-done.30
  538.0 0.7 convolution_add_fusion.3
  538.7 0.3 copy-done.18
  539.2 0.7 convolution_add_fusion.2
  539.9 0.3 copy-done.6
  540.4 0.7 convolution_add_fusion.1
  541.1 0.7 convolution_add_fusion
  542.1 0.5 convolution_bitcast_fusion
  542.6 2.1 fusion
  544.7 0.6 dynamic_slice.3
  545.3 114.5 %reduce-scatter.2.cloned.1.call-done = bf16[128,3,1024]{2,0,1:T(8,128)(2,1)} async-done(((bf16[128,3,4096]{2,0,1:T(8,128)(2,1)}), bf16[128,3,1024]{2,0,1:T(8,128)(2,1)}) %reduce-scatter.2.cloned.1.call-update) | async-done | bytes 786448 | tf_op jit(solution)/shard_map/reduce_scatter | solution.py:99
  659.8 1.2 slice.195
  661.0 1.8 copy.36
  663.0 0.8 slice_bitcast_fusion
  (92 shorter events, 3.3 us)
Async XLA Ops:
  7.2 164.0 %copy-start = (f32[64,4096]{1,0:T(8,128)S(1)}, f32[64,4096]{1,0:T(8,128)}, u32[]{:S(2)}) copy-start(f32[64,4096]{1,0:T(8,128)} %param.15) | copy-start | bytes 3145732
  7.2 173.2 %all-gather.3.cloned.1.call-start = ((), (), s32[]{:S(2)}) async-start(), calls=%async_computation.1 | async-start | bytes 1064960 | tf_op jit(solution)/shard_map/all_gather | solution.py:53
  7.9 651.9 %reduce-scatter.2.cloned.1.call-start = ((), (), s32[]{:S(2)}) async-start(), calls=%async_computation.2 | async-start | bytes 3932160 | tf_op jit(solution)/shard_map/reduce_scatter | solution.py:99
  171.2 0.9 copy-start.37
  171.2 1.6 copy-start.2
  180.4 6.8 %copy-start.4 = (bf16[16,8,2,4096]{3,1,2,0:T(8,128)(2,1)S(1)}, bf16[16,8,2,4096]{3,1,2,0:T(8,128)(2,1)}, u32[]{:S(2)}) copy-start(bf16[16,8,2,4096]{3,1,2,0:T(8,128)(2,1)} %copy.40) | copy-start | bytes 6291460
  187.1 0.9 copy-start.9
  187.1 9.9 %copy-start.11 = (bf16[64,4096]{1,0:T(8,128)(2,1)}, bf16[64,4096]{1,0:T(8,128)(2,1)S(1)}, u32[]{:S(2)}) copy-start(bf16[64,4096]{1,0:T(8,128)(2,1)S(1)} %get-tuple-element.36) | copy-start | bytes 1572868
  197.1 0.9 copy-start.13
  197.1 10.4 %copy-start.15 = (bf16[64,4096]{1,0:T(8,128)(2,1)}, bf16[64,4096]{1,0:T(8,128)(2,1)S(1)}, u32[]{:S(2)}) copy-start(bf16[64,4096]{1,0:T(8,128)(2,1)S(1)} %get-tuple-element.38) | copy-start | bytes 1572868
  207.5 0.9 copy-start.21
  207.5 9.9 %copy-start.23 = (bf16[64,4096]{1,0:T(8,128)(2,1)}, bf16[64,4096]{1,0:T(8,128)(2,1)S(1)}, u32[]{:S(2)}) copy-start(bf16[64,4096]{1,0:T(8,128)(2,1)S(1)} %get-tuple-element.40) | copy-start | bytes 1572868
  207.5 22.7 %copy-start.5 = (bf16[64,4096]{1,0:T(8,128)(2,1)}, bf16[64,4096]{1,0:T(8,128)(2,1)S(1)}, u32[]{:S(2)}) copy-start(bf16[64,4096]{1,0:T(8,128)(2,1)S(1)} %get-tuple-element.21) | copy-start | bytes 1572868
  207.6 22.7 %copy-start.7 = (bf16[64,4096]{1,0:T(8,128)(2,1)}, bf16[64,4096]{1,0:T(8,128)(2,1)S(1)}, u32[]{:S(2)}) copy-start(bf16[64,4096]{1,0:T(8,128)(2,1)S(1)} %get-tuple-element.22) | copy-start | bytes 1572868
  217.5 10.1 %copy-start.25 = (bf16[64,4096]{1,0:T(8,128)(2,1)}, bf16[64,4096]{1,0:T(8,128)(2,1)S(1)}, u32[]{:S(2)}) copy-start(bf16[64,4096]{1,0:T(8,128)(2,1)S(1)} %get-tuple-element.41) | copy-start | bytes 1572868
  217.5 10.1 %copy-start.27 = (bf16[64,4096]{1,0:T(8,128)(2,1)}, bf16[64,4096]{1,0:T(8,128)(2,1)S(1)}, u32[]{:S(2)}) copy-start(bf16[64,4096]{1,0:T(8,128)(2,1)S(1)} %get-tuple-element.42) | copy-start | bytes 1572868
  217.5 11.9 %copy-start.17 = (bf16[64,4096]{1,0:T(8,128)(2,1)}, bf16[64,4096]{1,0:T(8,128)(2,1)S(1)}, u32[]{:S(2)}) copy-start(bf16[64,4096]{1,0:T(8,128)(2,1)S(1)} %get-tuple-element.23) | copy-start | bytes 1572868
  217.5 11.9 %copy-start.19 = (bf16[64,4096]{1,0:T(8,128)(2,1)}, bf16[64,4096]{1,0:T(8,128)(2,1)S(1)}, u32[]{:S(2)}) copy-start(bf16[64,4096]{1,0:T(8,128)(2,1)S(1)} %get-tuple-element.24) | copy-start | bytes 1572868
  227.6 1.7 copy-start.29
  227.6 1.7 copy-start.31
  227.6 1.7 copy-start.33
  227.6 1.7 copy-start.35
  231.1 0.9 copy-start.38
  231.1 300.8 %copy-start.10 = (bf16[64,4096]{1,0:T(8,128)(2,1)S(1)}, bf16[64,4096]{1,0:T(8,128)(2,1)}, u32[]{:S(2)}) copy-start(bf16[64,4096]{1,0:T(8,128)(2,1)} %copy-done.9) | copy-start | bytes 1572868
  231.1 300.8 %copy-start.12 = (bf16[64,4096]{1,0:T(8,128)(2,1)S(1)}, bf16[64,4096]{1,0:T(8,128)(2,1)}, u32[]{:S(2)}) copy-start(bf16[64,4096]{1,0:T(8,128)(2,1)} %copy-done.11) | copy-start | bytes 1572868
  532.0 1.0 copy-start.14
  532.0 1.2 copy-start.16
  533.2 1.0 copy-start.22
  533.2 1.2 copy-start.24
  534.4 1.0 copy-start.26
  534.4 1.2 copy-start.28
  535.6 1.0 copy-start.34
  535.6 1.2 copy-start.36
  536.8 1.0 copy-start.30
  536.8 1.2 copy-start.32
  538.0 1.0 copy-start.18
  538.0 1.2 copy-start.20
  539.2 1.0 copy-start.6
  539.2 1.2 copy-start.8
  659.8 3.0 copy-start.3
  661.0 2.8 copy-start.1
Sparse Core Ops, SparseCore 0:
  11.5 113.1 all-gather.2
  544.8 114.8 reduce-scatter.1
where the time goes:
time: 674 us; the launch traced here: 671 us
  blocking collectives  456 us (68%)
  waiting for transfers between devices  115 us (17%)
  other arithmetic  47.3 us (7%)
  matrix products  18.3 us (3%)
  local copies, waits for them, and re-layouts  18.1 us (3%)
  between operations  16.2 us (2%)
    all_gather x1, blocking collectives, on_device(): lax.all_gather(meta, 'orient', axis=0, tiled=True)  157 us
    psum x1, blocking collectives, on_device(): lax.psum(jnp.sum(jnp.exp(score - top[None, :, None]), axis=(0, 2)), 'orie...  151 us
    pmax x1, blocking collectives, on_device(): top = lax.pmax(local_top, 'orient')  149 us
    reduce_scatter x1, waiting for transfers between devices, on_device(): lax.psum_scatter(stacked.astype(jnp.bfloat16), 'dom', scatter_dimension=2...  114 us
    another operation x6, other arithmetic  42.2 us
  transfers between devices with their start and end apart: 2, of which 1 were waited for; matrix products, arithmetic and copies ran while one was open for 2% of the time, Pallas kernels for 0%

commit v1 on v0

--- a/solution.py
+++ b/solution.py
@@ -80,7 +80,8 @@
     score = cross - 0.5 * self_term[None, :, :] + prior.T[:, :, None] + log_prior[None, None, :]
     local_top = jnp.max(score, axis=(0, 2))
     top = lax.pmax(local_top, "orient")
-    mass = lax.psum(jnp.sum(jnp.exp(score - top[None, :, None]), axis=(0, 2)), "orient")
+    view = jnp.sum(jnp.exp(score - top[None, :, None]), axis=(0, 2))
+    mass = jnp.sum(lax.all_gather(view, "orient"), axis=0)
     evidence = top + jnp.log(mass)
     post = jnp.exp(score - evidence[None, :, None]).astype(jnp.bfloat16)
     post_sum = jnp.sum(post.astype(jnp.float32), axis=0).astype(jnp.bfloat16)

time: 674 us -> 850 us (1.26)
  blocking collectives: 456 us -> 603 us
  waiting for transfers between devices: 115 us -> 143 us
    unnamed x0 -> x1, blocking collectives: none -> 297 us
    psum x1 -> x0, blocking collectives: 151 us -> none  [on_device(): lax.psum(jnp.sum(jnp.exp(score - top[None, :, None]), axis=(0, 2)), 'orie...]
    reduce_scatter x1, waiting for transfers between devices: 114 us -> 142 us  [on_device(): lax.psum_scatter(stacked.astype(jnp.bfloat16), 'dom', scatter_dimension=2...]
where the time goes in v1:
time: 850 us; the launch traced here: 847 us
  blocking collectives  603 us (71%)
  waiting for transfers between devices  143 us (17%)
  other arithmetic  47.3 us (6%)
  local copies, waits for them, and re-layouts  19 us (2%)
  matrix products  18.3 us (2%)
  between operations  16.9 us (2%)
    unnamed x1, blocking collectives  297 us
    all_gather x1, blocking collectives, on_device(): lax.all_gather(meta, 'orient', axis=0, tiled=True)  157 us
    pmax x1, blocking collectives, on_device(): top = lax.pmax(local_top, 'orient')  149 us
    reduce_scatter x1, waiting for transfers between devices, on_device(): lax.psum_scatter(stacked.astype(jnp.bfloat16), 'dom', scatter_dimension=2...  142 us
    another operation x6, other arithmetic  42.2 us
  transfers between devices with their start and end apart: 2, of which 1 were waited for; matrix products, arithmetic and copies ran while one was open for 2% of the time, Pallas kernels for 0%

profile of v1, /device:TPU:1, one launch (start us, length us, event | category | flops | bytes accessed | tf_op | source)
XLA Modules:
  0.0 846.9 jit_solution(13477488853204897887)
XLA Ops:
  7.2 0.7 all-gather.4.cloned.1.call-update
  8.0 0.7 convert.69
  10.2 156.5 %all-gather.1 = bf16[64,1,20]{2,1,0:T(2,128)(2,1)S(1)} all-gather(bf16[1,1,20]{2,1,0:T(2,128)(2,1)S(1)} %maximum_bitcast_fusion), channel_id=1, replica_groups=mesh['orient'=64,'dom'=4] {'orient'}, dimensions={0}, use_global_device_ids=true | all-gather | bytes 2600 | tf_op jit(solution)/shard_map/all_gather | solution.py:54
  167.0 4.2 copy.47
  171.2 0.6 dynamic-slice
  172.5 0.6 fusion.97
  173.1 0.6 multiply_convert_fusion.1
  174.0 5.1 fusion.130
  179.1 2.4 convolution_multiply_fusion.1
  181.6 2.0 multiply_convert_fusion
  183.6 4.7 fusion.40
  188.3 0.9 fusion.9
  189.2 9.0 %fusion.72 = (bf16[64,4096]{1,0:T(8,128)(2,1)S(1)}, bf16[64,4096]{1,0:T(8,128)(2,1)S(1)}, bf16[64,4096]{1,0:T(8,128)(2,1)S(1)}, bf16[64,4096]{1,0:T(8,128)(2,1)S(1)}) fusion(s32[4096]{0:T(1024)S(1)} %get-tuple-element.71, s32[64]{0:T(128)S(1)} %get-tuple-element.59, s32[4096]{0:T(1024)S(1)} %get-tuple-element.70, s32[64]{0:T(128)S(1)} %get-tuple-element.80, ...), kind=kLoop, calls=%fused_computation.158 | loop fusion | flops 13107200 | bytes 3179520 | tf_op jit(solution)/shard_map/convert.3
  198.3 0.8 fusion.8
  199.1 9.6 %fusion.68 = (bf16[64,4096]{1,0:T(8,128)(2,1)S(1)}, bf16[64,4096]{1,0:T(8,128)(2,1)S(1)}, bf16[64,4096]{1,0:T(8,128)(2,1)S(1)}, bf16[64,4096]{1,0:T(8,128)(2,1)S(1)}) fusion(s32[4096]{0:T(1024)S(1)} %get-tuple-element.71, s32[64]{0:T(128)S(1)} %get-tuple-element.60, s32[4096]{0:T(1024)S(1)} %get-tuple-element.70, s32[64]{0:T(128)S(1)} %get-tuple-element.79, ...), kind=kLoop, calls=%fused_computation.154 | loop fusion | flops 13107200 | bytes 3179520 | tf_op jit(solution)/shard_map/convert.5
  208.7 0.8 fusion.7
  209.6 9.0 %fusion.64 = (bf16[64,4096]{1,0:T(8,128)(2,1)S(1)}, bf16[64,4096]{1,0:T(8,128)(2,1)S(1)}, bf16[64,4096]{1,0:T(8,128)(2,1)S(1)}, bf16[64,4096]{1,0:T(8,128)(2,1)S(1)}) fusion(s32[4096]{0:T(1024)S(1)} %get-tuple-element.71, s32[64]{0:T(128)S(1)} %get-tuple-element.61, s32[4096]{0:T(1024)S(1)} %get-tuple-element.70, s32[64]{0:T(128)S(1)} %get-tuple-element.78, ...), kind=kLoop, calls=%fused_computation.150 | loop fusion | flops 13107200 | bytes 3179520 | tf_op jit(solution)/shard_map/convert.7
  218.7 0.8 fusion.6
  219.6 9.2 %fusion.60 = (bf16[64,4096]{1,0:T(8,128)(2,1)S(1)}, bf16[64,4096]{1,0:T(8,128)(2,1)S(1)}, bf16[64,4096]{1,0:T(8,128)(2,1)S(1)}, bf16[64,4096]{1,0:T(8,128)(2,1)S(1)}) fusion(s32[4096]{0:T(1024)S(1)} %get-tuple-element.71, s32[64]{0:T(128)S(1)} %get-tuple-element.62, s32[4096]{0:T(1024)S(1)} %get-tuple-element.70, s32[64]{0:T(128)S(1)} %get-tuple-element.77, ...), kind=kLoop, calls=%fused_computation.146 | loop fusion | flops 13107200 | bytes 3179520 | tf_op jit(solution)/shard_map/convert.9
  228.8 0.8 fusion.5
  229.7 0.8 fusion.4
  230.6 0.8 fusion.3
  231.5 0.8 fusion.2
  232.3 0.9 fusion.1
  233.5 148.6 %pmax.7 = f32[64]{0:T(128)S(1)} all-reduce(f32[64]{0:T(128)S(1)} %fusion.96), channel_id=1, replica_groups=mesh['orient'=64,'dom'=4] {'orient'}, use_global_device_ids=true, to_apply=%region_1.2 | all-reduce | flops 64 | bytes 512 | tf_op jit(solution)/shard_map/pmax | solution.py:82
  382.7 297.4 %all-reduce = f32[4096]{0:T(1024)S(1)} all-reduce(f32[4096]{0:T(1024)S(1)} %dynamic-update-slice), channel_id=2, replica_groups=mesh['orient'=64,'dom'=4] {'orient'}, use_global_device_ids=true, to_apply=%add | all-reduce | flops 4096 | bytes 32768
  680.4 0.7 fusion.77
  681.6 0.7 convolution_add_fusion.7
  682.4 0.3 copy-done.22
  682.8 0.7 convolution_add_fusion.6
  683.6 0.3 copy-done.26
  684.0 0.7 convolution_add_fusion.5
  684.8 0.3 copy-done.34
  685.2 0.7 convolution_add_fusion.4
  686.0 0.3 copy-done.30
  686.4 0.7 convolution_add_fusion.3
  687.2 0.3 copy-done.18
  687.6 0.7 convolution_add_fusion.2
  688.4 0.3 copy-done.6
  688.8 0.7 convolution_add_fusion.1
  689.6 0.7 convolution_add_fusion
  690.6 0.5 convolution_bitcast_fusion
  691.1 2.1 fusion
  693.2 0.6 dynamic_slice.3
  693.8 142.0 %reduce-scatter.2.cloned.1.call-done = bf16[128,3,1024]{2,0,1:T(8,128)(2,1)} async-done(((bf16[128,3,4096]{2,0,1:T(8,128)(2,1)}), bf16[128,3,1024]{2,0,1:T(8,128)(2,1)}) %reduce-scatter.2.cloned.1.call-update) | async-done | bytes 786448 | tf_op jit(solution)/shard_map/reduce_scatter | solution.py:100
  835.8 1.2 slice.195
  837.0 1.8 copy.43
  839.0 0.8 slice_bitcast_fusion
  (99 shorter events, 3.9 us)
Async XLA Ops:
  7.2 165.3 %copy-start = (f32[64,4096]{1,0:T(8,128)S(1)}, f32[64,4096]{1,0:T(8,128)}, u32[]{:S(2)}) copy-start(f32[64,4096]{1,0:T(8,128)} %param.15) | copy-start | bytes 3145732
  7.2 174.4 %all-gather.4.cloned.1.call-start = ((), (), s32[]{:S(2)}) async-start(), calls=%async_computation.1 | async-start | bytes 1064960 | tf_op jit(solution)/shard_map/all_gather | solution.py:53
  7.9 827.9 %reduce-scatter.2.cloned.1.call-start = ((), (), s32[]{:S(2)}) async-start(), calls=%async_computation.2 | async-start | bytes 3932160 | tf_op jit(solution)/shard_map/reduce_scatter | solution.py:100
  166.9 4.2 copy-start.39
  171.2 1.9 copy-start.37
  172.4 1.6 copy-start.2
  181.6 6.8 copy-start.4
  188.3 0.9 copy-start.9
  188.3 9.9 %copy-start.11 = (bf16[64,4096]{1,0:T(8,128)(2,1)}, bf16[64,4096]{1,0:T(8,128)(2,1)S(1)}, u32[]{:S(2)}) copy-start(bf16[64,4096]{1,0:T(8,128)(2,1)S(1)} %get-tuple-element.39) | copy-start | bytes 1572868
  198.2 0.9 copy-start.13
  198.3 10.4 %copy-start.15 = (bf16[64,4096]{1,0:T(8,128)(2,1)}, bf16[64,4096]{1,0:T(8,128)(2,1)S(1)}, u32[]{:S(2)}) copy-start(bf16[64,4096]{1,0:T(8,128)(2,1)S(1)} %get-tuple-element.41) | copy-start | bytes 1572868
  208.7 0.9 copy-start.21
  208.7 9.9 %copy-start.23 = (bf16[64,4096]{1,0:T(8,128)(2,1)}, bf16[64,4096]{1,0:T(8,128)(2,1)S(1)}, u32[]{:S(2)}) copy-start(bf16[64,4096]{1,0:T(8,128)(2,1)S(1)} %get-tuple-element.43) | copy-start | bytes 1572868
  208.7 22.7 %copy-start.5 = (bf16[64,4096]{1,0:T(8,128)(2,1)}, bf16[64,4096]{1,0:T(8,128)(2,1)S(1)}, u32[]{:S(2)}) copy-start(bf16[64,4096]{1,0:T(8,128)(2,1)S(1)} %get-tuple-element.24) | copy-start | bytes 1572868
  208.7 22.7 %copy-start.7 = (bf16[64,4096]{1,0:T(8,128)(2,1)}, bf16[64,4096]{1,0:T(8,128)(2,1)S(1)}, u32[]{:S(2)}) copy-start(bf16[64,4096]{1,0:T(8,128)(2,1)S(1)} %get-tuple-element.25) | copy-start | bytes 1572868
  218.7 10.1 %copy-start.25 = (bf16[64,4096]{1,0:T(8,128)(2,1)}, bf16[64,4096]{1,0:T(8,128)(2,1)S(1)}, u32[]{:S(2)}) copy-start(bf16[64,4096]{1,0:T(8,128)(2,1)S(1)} %get-tuple-element.44) | copy-start | bytes 1572868
  218.7 10.1 %copy-start.27 = (bf16[64,4096]{1,0:T(8,128)(2,1)}, bf16[64,4096]{1,0:T(8,128)(2,1)S(1)}, u32[]{:S(2)}) copy-start(bf16[64,4096]{1,0:T(8,128)(2,1)S(1)} %get-tuple-element.45) | copy-start | bytes 1572868
  218.7 11.9 %copy-start.17 = (bf16[64,4096]{1,0:T(8,128)(2,1)}, bf16[64,4096]{1,0:T(8,128)(2,1)S(1)}, u32[]{:S(2)}) copy-start(bf16[64,4096]{1,0:T(8,128)(2,1)S(1)} %get-tuple-element.26) | copy-start | bytes 1572868
  218.7 11.9 %copy-start.19 = (bf16[64,4096]{1,0:T(8,128)(2,1)}, bf16[64,4096]{1,0:T(8,128)(2,1)S(1)}, u32[]{:S(2)}) copy-start(bf16[64,4096]{1,0:T(8,128)(2,1)S(1)} %get-tuple-element.27) | copy-start | bytes 1572868
  228.8 1.7 copy-start.29
  228.8 1.7 copy-start.31
  228.8 1.7 copy-start.33
  228.8 1.7 copy-start.35
  232.3 0.9 copy-start.38
  232.3 448.1 %copy-start.10 = (bf16[64,4096]{1,0:T(8,128)(2,1)S(1)}, bf16[64,4096]{1,0:T(8,128)(2,1)}, u32[]{:S(2)}) copy-start(bf16[64,4096]{1,0:T(8,128)(2,1)} %copy-done.9) | copy-start | bytes 1572868
  232.3 448.1 %copy-start.12 = (bf16[64,4096]{1,0:T(8,128)(2,1)S(1)}, bf16[64,4096]{1,0:T(8,128)(2,1)}, u32[]{:S(2)}) copy-start(bf16[64,4096]{1,0:T(8,128)(2,1)} %copy-done.11) | copy-start | bytes 1572868
  680.4 1.0 copy-start.14
  680.4 1.2 copy-start.16
  681.6 1.0 copy-start.22
  681.6 1.2 copy-start.24
  682.8 1.0 copy-start.26
  682.8 1.2 copy-start.28
  684.0 1.0 copy-start.34
  684.0 1.2 copy-start.36
  685.2 1.0 copy-start.30
  685.2 1.2 copy-start.32
  686.4 1.0 copy-start.18
  686.4 1.2 copy-start.20
  687.6 1.0 copy-start.6
  687.6 1.2 copy-start.8
  835.8 3.0 copy-start.3
  837.0 2.8 copy-start.1
Sparse Core Ops, SparseCore 0:
  11.5 113.1 all-gather.3
  693.3 142.4 reduce-scatter.1
